TPU v7x, 32 devices: a whole 2x2x4 slice. The times are simulated.
32 devices in a mesh: req: 2 (over x), vocab: 16 (over z, y, core).
Axes of the slice: x: 2, y: 2, z: 4, core: 2. Of those that a mesh axis runs over, the one named last changes fastest.
Arguments:
- hidden: bfloat16 [512, 2304], P(('req', 'vocab'))
- norm_gain: float32 [2304], replicated, may hold values from 0.5 to 1.5
- head_weight: bfloat16 [2304, 16384], P(None, 'vocab')
- targets: int32 [512], P(('req', 'vocab')), may hold values from 0 to 16383
- counts: int32 [32], P(('req', 'vocab')), may hold values from 5 to 10, as said below
Outputs:
- logprob: float32 [512], P(('req', 'vocab'))
- entropy: float32 [512], P(('req', 'vocab'))
Inputs may be any that keep to these rules, and one draw needn't show every extreme that they name: The scored slots of a device are its first counts slots; some device holds exactly 10.
All inputs are finite; a program needn't handle non-finite values.
Results may differ from a plain program's by a relative error of at most 0.012.
The roundings to bfloat16 on the way count: a program that leaves them out, or rounds other values in their place, can miss the bound.
Values may be sent and summed in bfloat16 or wider, within the bound.
No kernel may reach another device: no remote copies, remote signals or barrier semaphores. Data moves between devices by JAX's collectives and lax.ppermute only.
A program may use at most 64 MiB of HBM per device.

v0:
```python
import jax
import jax.numpy as jnp
from jax import lax
from jax.sharding import PartitionSpec as P

logit_scale = 256.0 / 2304.0


def on_device(hidden, norm_gain, head_weight, targets, counts):
    slots = hidden.shape[0]
    vocab_dev = head_weight.shape[1]
    values = hidden.astype(jnp.float32)
    square_mean = jnp.mean(values * values, axis=1, keepdims=True)
    normed = (values * lax.rsqrt(square_mean + 1e-05) * norm_gain[None, :]).astype(jnp.bfloat16)
    gathered = lax.all_gather(normed, "vocab", axis=0, tiled=True)
    wanted = lax.all_gather(targets, "vocab", axis=0, tiled=True)
    position = lax.axis_index("vocab")
    start = position * vocab_dev
    logits = jnp.dot(gathered, head_weight, preferred_element_type=jnp.float32) * logit_scale
    local_peak = jnp.max(logits, axis=1)
    weights = jnp.exp(logits - local_peak[:, None])
    local_total = jnp.sum(weights, axis=1)
    local_moment = jnp.sum(weights * logits, axis=1)
    columns = lax.broadcasted_iota(jnp.int32, logits.shape, 1)
    hits = columns == (wanted - start)[:, None]
    local_chosen = jnp.sum(jnp.where(hits, logits, jnp.float32(0.0)), axis=1)
    own_start = position * slots
    peak = lax.pmax(local_peak, "vocab")
    factor = jnp.exp(local_peak - peak)
    total, moment, chosen = lax.psum(
        (local_total * factor, local_moment * factor, local_chosen), "vocab"
    )
    peak = lax.dynamic_slice_in_dim(peak, own_start, slots, 0)
    total = lax.dynamic_slice_in_dim(total, own_start, slots, 0)
    moment = lax.dynamic_slice_in_dim(moment, own_start, slots, 0)
    chosen = lax.dynamic_slice_in_dim(chosen, own_start, slots, 0)
    log_total = jnp.log(total)
    row_logprob = chosen - peak - log_total
    row_entropy = peak + log_total - moment / total
    scored = jnp.arange(slots, dtype=jnp.int32) < counts[0]
    logprob = jnp.where(scored, row_logprob, jnp.float32(0.0))
    entropy = jnp.where(scored, row_entropy, jnp.float32(0.0))
    return (logprob, entropy)


def solution(mesh):
    in_specs = (
        P(("req", "vocab"), None),
        P(),
        P(None, "vocab"),
        P(("req", "vocab")),
        P(("req", "vocab")),
    )
    out_specs = (P(("req", "vocab")), P(("req", "vocab")))
    return jax.shard_map(
        on_device, mesh=mesh, in_specs=in_specs, out_specs=out_specs, check_vma=False
    )
```

profile of v0, /device:TPU:0, one launch (start us, length us, event | category | flops | bytes accessed | tf_op | source)
XLA Modules:
  0.0 124.6 jit_solution(5613931167533557887)
XLA Ops:
  7.2 0.0 all-gather.2.cloned.1.call-start
  7.2 1.0 fusion.1
  8.2 1.6 %fusion.3 = bf16[16,2304]{1,0:T(8,128)(2,1)} fusion(bf16[16,2304]{1,0:T(8,128)(2,1)} %param.5, f32[2304]{0:T(1024)} %param.6, f32[16]{0:T(128)S(1)} %add_rsqrt_fusion), kind=kLoop, calls=%fused_computation.10 | loop fusion | flops 147456 | bytes 156736 | tf_op jit(solution)/shard_map/convert_element_type | solution.py:14
  9.8 0.0 all-gather.2.cloned.1.call-update
  10.5 1.2 dynamic-slice
  12.4 0.9 dynamic-update-slice
  13.3 13.7 %all-reduce = s32[256]{0:T(256)S(1)} all-reduce(s32[256]{0:T(256)S(1)} %dynamic-update-slice), channel_id=1, replica_groups=mesh['req'=2,'vocab'=16] {'vocab'}, use_global_device_ids=true, to_apply=%add | all-reduce | flops 256 | bytes 2048
  27.0 24.3 %all-gather.2.cloned.1.call-done = bf16[256,2304]{1,0:T(8,128)(2,1)} async-done(((bf16[16,2304]{1,0:T(8,128)(2,1)}), bf16[256,2304]{1,0:T(8,128)(2,1)}) %all-gather.2.cloned.1.call-update) | async-done | bytes 1179664 | tf_op jit(solution)/shard_map/all_gather | solution.py:15
  51.3 4.2 %fusion.6 = (f32[256]{0:T(256)S(1)}, f32[256,1024]{1,0:T(8,128)S(1)}) fusion(bf16[256,2304]{1,0:T(8,128)(2,1)} %all-gather.2.cloned.1.call-done, bf16[2304,1024]{1,0:T(8,128)(2,1)} %param.7), kind=kOutput, calls=%fused_computation.18 | convolution fusion | flops 1208483584 | bytes 6947840 | tf_op jit(solution)/shard_map/dot_general | solution.py:19
  55.5 31.7 %pmax.7 = f32[256]{0:T(256)S(1)} all-reduce(f32[256]{0:T(256)S(1)} %get-tuple-element.12), channel_id=1, replica_groups=mesh['req'=2,'vocab'=16] {'vocab'}, use_global_device_ids=true, to_apply=%region_4.5 | all-reduce | flops 256 | bytes 2048 | tf_op jit(solution)/shard_map/pmax | solution.py:28
  87.2 0.5 multiply_reduce_fusion
  87.7 29.5 %all-reduce.1 = (f32[256]{0:T(256)S(1)}, f32[256]{0:T(256)S(1)}, f32[256]{0:T(256)S(1)}) all-reduce(f32[256]{0:T(256)S(1)} %get-tuple-element.4, f32[256]{0:T(256)S(1)} %get-tuple-element.11, f32[256]{0:T(256)S(1)} %get-tuple-element.10), channel_id=1, replica_groups=mesh['req'=2,'vocab'=16] {'vocab'}, use_global_device_ids=true, to_apply=%region_2.0 | all-reduce | flops 768 | bytes 6144 | tf_op jit(solution)/shard_map/psum | solution.py:30
  117.2 0.6 compare_select_fusion
  (4 shorter events, 0.0 us)
Async XLA Ops:
  7.2 44.2 %all-gather.2.cloned.1.call-start = ((), (), s32[]{:S(2)}) async-start(), calls=%async_computation | async-start | bytes 1253376 | tf_op jit(solution)/shard_map/all_gather | solution.py:15
Sparse Core Ops, SparseCore 0:
  10.3 41.0 all-gather.1
where the time goes:
time: 125 us
  blocking collectives  74.9 us (60%)
  waiting for transfers between devices  24.3 us (19%)
  between operations  15.3 us (12%)
  matrix products  4.18 us (3%)
  other arithmetic  3.73 us (3%)
  local copies, waits for them, and re-layouts  2.1 us (2%)
    pmax x1, blocking collectives, on_device(): peak = lax.pmax(local_peak, 'vocab')  31.7 us
    psum x1, blocking collectives, on_device(): lax.psum((local_total * factor, local_moment * factor, local_chosen), 'vo...  29.5 us
    all_gather x1, waiting for transfers between devices, on_device(): gathered = lax.all_gather(normed, 'vocab', axis=0, tiled=True)  24.3 us
    unnamed x1, blocking collectives  13.7 us
    dot_general x1, matrix products, on_device(): jnp.dot(gathered, head_weight, preferred_element_type=jnp.float32)  4.18 us
  transfers between devices with their start and end apart: 1, of which 1 were waited for; matrix products, arithmetic and copies ran while one was open for 2% of the time, Pallas kernels for 0%

commit v1 on v0

v1 whole, which is shorter than its diff:
```python
import jax
import jax.numpy as jnp
from jax import lax
from jax.sharding import PartitionSpec as P

logit_scale = 256.0 / 2304.0


def gather_masks(n):
    if n == 16:
        return [[5, 8, 13], [3], [1]]
    steps, bit = [], n // 2
    while bit:
        steps.append([bit])
        bit //= 2
    return steps


def swap(block, mask, n):
    return lax.ppermute(block, "vocab", [(i, i ^ mask) for i in range(n)])


def gather(block, n):
    blocks, owners = [block], [0]
    for masks in gather_masks(n):
        if len(blocks) == n // 2:
            whole = jnp.concatenate([jnp.stack(blocks)])
            got = swap(whole, masks[0], n)
            return jnp.concatenate([whole, got]), owners + [o ^ masks[0] for o in owners]
        got = [swap(b, mask, n) for mask in masks for b in blocks]
        owners = owners + [o ^ mask for mask in masks for o in owners]
        blocks = blocks + got
    return jnp.stack(blocks), owners


def on_device(n, hidden, norm_gain, head_weight, targets, counts):
    slots, width = hidden.shape
    vocab_dev = head_weight.shape[1]
    values = hidden.astype(jnp.float32)
    square_mean = jnp.mean(values * values, axis=1, keepdims=True)
    normed = (values * lax.rsqrt(square_mean + 1e-05) * norm_gain[None, :]).astype(jnp.bfloat16)
    ids = jnp.stack([targets // 256, targets % 256], axis=1).astype(jnp.bfloat16)
    payload = jnp.concatenate([normed, jnp.pad(ids, ((0, 0), (0, 126)))], axis=1)
    blocks, owners = gather(payload, n)
    rows = blocks.reshape(n * slots, width + 128)
    gathered = rows[:, :width]
    ids = rows[:, width:width + 2].astype(jnp.int32)
    wanted = ids[:, 0] * 256 + ids[:, 1]
    position = lax.axis_index("vocab")
    logits = jnp.dot(gathered, head_weight, preferred_element_type=jnp.float32) * logit_scale
    local_peak = jnp.max(logits, axis=1)
    weights = jnp.exp(logits - local_peak[:, None])
    local_total = jnp.sum(weights, axis=1)
    local_moment = jnp.sum(weights * logits, axis=1)
    columns = lax.broadcasted_iota(jnp.int32, logits.shape, 1)
    hits = columns == (wanted - position * vocab_dev)[:, None]
    local_chosen = jnp.sum(jnp.where(hits, logits, jnp.float32(0.0)), axis=1)
    stats = jnp.stack([local_peak, local_total, local_moment, local_chosen]).reshape(4, n, slots)
    owner_of = jnp.array(owners, jnp.int32) ^ position
    one_hot = jnp.arange(n, dtype=jnp.int32)[:, None] == owner_of[None, :]
    placed = jnp.sum(jnp.where(one_hot[:, :, None, None], stats.transpose(1, 0, 2)[None], 0.0), axis=1)
    back = lax.all_to_all(placed, "vocab", 0, 0, tiled=True)
    peaks, totals, moments, chosens = back[:, 0], back[:, 1], back[:, 2], back[:, 3]
    peak = jnp.max(peaks, axis=0)
    factor = jnp.exp(peaks - peak[None])
    total = jnp.sum(totals * factor, axis=0)
    moment = jnp.sum(moments * factor, axis=0)
    chosen = jnp.sum(chosens, axis=0)
    log_total = jnp.log(total)
    scored = jnp.arange(slots, dtype=jnp.int32) < counts[0]
    logprob = jnp.where(scored, chosen - peak - log_total, jnp.float32(0.0))
    entropy = jnp.where(scored, peak + log_total - moment / total, jnp.float32(0.0))
    return (logprob, entropy)


def solution(mesh):
    n = mesh.shape["vocab"]
    in_specs = (
        P(("req", "vocab"), None),
        P(),
        P(None, "vocab"),
        P(("req", "vocab")),
        P(("req", "vocab")),
    )
    out_specs = (P(("req", "vocab")), P(("req", "vocab")))

    def step(*args):
        return on_device(n, *args)

    return jax.shard_map(step, mesh=mesh, in_specs=in_specs, out_specs=out_specs, check_vma=False)
```

time: 125 us -> 41.6 us (0.33)
  blocking collectives: 74.9 us -> 0 us
  between operations: 15.3 us -> 1.39 us
  starting transfers between devices: 0.04 us -> 13.9 us
  waiting for transfers between devices: 24.3 us -> 16.8 us
  local copies, waits for them, and re-layouts: 2.1 us -> 0.73 us
    pmax x1 -> x0, blocking collectives: 31.7 us -> none  [on_device(): peak = lax.pmax(local_peak, 'vocab')]
    psum x1 -> x0, blocking collectives: 29.5 us -> none  [on_device(): lax.psum((local_total * factor, local_moment * factor, local_chosen), 'vo...]
    all_gather x1 -> x0, waiting for transfers between devices: 24.3 us -> none  [on_device(): gathered = lax.all_gather(normed, 'vocab', axis=0, tiled=True)]
    unnamed x1 -> x0, blocking collectives: 13.7 us -> none
    ppermute x0 -> x8, waiting for transfers between devices: none -> 10.8 us  [swap(): return lax.ppermute(block, 'vocab', [(i, i ^ mask) for i in range(n)])]
    ppermute x0 -> x8, starting transfers between devices: none -> 9.18 us  [swap(): return lax.ppermute(block, 'vocab', [(i, i ^ mask) for i in range(n)])]
    all_to_all x0 -> x1, waiting for transfers between devices: none -> 5.99 us  [on_device(): back = lax.all_to_all(placed, 'vocab', 0, 0, tiled=True)]
    all_to_all x0 -> x1, starting transfers between devices: none -> 4.74 us  [on_device(): back = lax.all_to_all(placed, 'vocab', 0, 0, tiled=True)]
  transfers between devices with their start and end apart: 1 -> 9, of which waited for: 1 -> 5; matrix products, arithmetic and copies ran while one was open for 2% -> 0% of each run, Pallas kernels for 0% -> 0%
where the time goes in v1:
time: 41.6 us; the launch traced here: 41.3 us
  waiting for transfers between devices  16.8 us (40%)
  starting transfers between devices  13.9 us (33%)
  other arithmetic  4.69 us (11%)
  matrix products  3.81 us (9%)
  between operations  1.39 us (3%)
  local copies, waits for them, and re-layouts  0.73 us (2%)
    ppermute x8, waiting for transfers between devices, swap(): return lax.ppermute(block, 'vocab', [(i, i ^ mask) for i in range(n)])  10.8 us
    ppermute x8, starting transfers between devices, swap(): return lax.ppermute(block, 'vocab', [(i, i ^ mask) for i in range(n)])  9.18 us
    all_to_all x1, waiting for transfers between devices, on_device(): back = lax.all_to_all(placed, 'vocab', 0, 0, tiled=True)  5.99 us
    all_to_all x1, starting transfers between devices, on_device(): back = lax.all_to_all(placed, 'vocab', 0, 0, tiled=True)  4.74 us
    dot_general x1, matrix products, on_device(): jnp.dot(gathered, head_weight, preferred_element_type=jnp.float32)  3.81 us
    reduce_sum x1, other arithmetic, on_device(): square_mean = jnp.mean(values * values, axis=1, keepdims=True)  1.02 us
    convert_element_type x1, other arithmetic, on_device(): (values * lax.rsqrt(square_mean + 1e-05) * norm_gain[None, :]).astype(jnp...  0.98 us
  transfers between devices with their start and end apart: 9, of which 5 were waited for; matrix products, arithmetic and copies ran while one was open for 0% of the time, Pallas kernels for 0%

profile of v1, /device:TPU:0, one launch (start us, length us, event | category | flops | bytes accessed | tf_op | source)
XLA Modules:
  0.0 41.3 jit_solution(6305022433784279332)
XLA Ops:
  0.6 0.7 %convert_bitcast_fusion = (bf16[16,1]{0,1:T(2,128)(2,1)S(1)}, bf16[16,1]{0,1:T(2,128)(2,1)S(1)}) fusion(s32[16]{0:T(128)} %param.9), kind=kLoop, calls=%fused_computation.51 | loop fusion | flops 336 | bytes 128 | tf_op jit(solution)/shard_map/stack | solution.py:42
  1.3 0.1 copy.23
  1.4 1.0 %fusion.3 = f32[16]{0:T(128)S(1)} fusion(bf16[16,2304]{1,0:T(8,128)(2,1)} %param.6), kind=kLoop, calls=%fused_computation.12 | loop fusion | flops 110576 | bytes 73792 | tf_op jit(solution)/shard_map/reduce_sum | solution.py:40
  2.5 1.0 %fusion.5 = bf16[16,2304]{1,0:T(8,128)(2,1)S(1)} fusion(bf16[16,2304]{1,0:T(8,128)(2,1)} %param.6, f32[2304]{0:T(1024)} %param.7, f32[16]{0:T(128)S(1)} %add_rsqrt_fusion), kind=kLoop, calls=%fused_computation.14 | loop fusion | flops 147456 | bytes 156736 | tf_op jit(solution)/shard_map/convert_element_type | solution.py:41
  3.4 2.5 %collective-permute-start = (bf16[16,2432]{1,0:T(8,128)(2,1)S(1)}, bf16[16,2432]{1,0:T(8,128)(2,1)S(1)}, u32[]{:S(2)}, u32[]{:S(2)}) collective-permute-start(bf16[16,2432]{1,0:T(8,128)(2,1)S(1)} %fusion.6), channel_id=1, source_target_pairs={{0,5},{1,4},{2,7},{3,6},{4,1},{5,0},{6,3},{7,2},{8,13},{9,12},{10,... | collective-permute-start | bytes 233480 | tf_op jit(solution)/shard_map/ppermute | solution.py:20
  6.0 2.6 %collective-permute-start.1 = (bf16[16,2432]{1,0:T(8,128)(2,1)S(1)}, bf16[16,2432]{1,0:T(8,128)(2,1)S(1)}, u32[]{:S(2)}, u32[]{:S(2)}) collective-permute-start(bf16[16,2432]{1,0:T(8,128)(2,1)S(1)} %fusion.6), channel_id=1, source_target_pairs={{0,8},{1,9},{2,10},{3,11},{4,12},{5,13},{6,14},{7,15},{8,0},{9,1},... | collective-permute-start | bytes 233480 | tf_op jit(solution)/shard_map/ppermute | solution.py:20
  8.6 0.2 collective-permute-start.2
  8.7 1.5 %collective-permute-start.3 = (bf16[16,2432]{1,0:T(8,128)(2,1)S(1)}, bf16[16,2432]{1,0:T(8,128)(2,1)S(1)}, u32[]{:S(2)}, u32[]{:S(2)}) collective-permute-start(bf16[16,2432]{1,0:T(8,128)(2,1)S(1)} %fusion.6), channel_id=1, source_target_pairs={{0,3},{1,2},{2,1},{3,0},{4,7},{5,6},{6,5},{7,4},{8,11},{9,10},{10,... | collective-permute-start | bytes 233480 | tf_op jit(solution)/shard_map/ppermute | solution.py:20
  10.2 0.5 %collective-permute-start.4 = (bf16[16,2432]{1,0:T(8,128)(2,1)S(1)}, bf16[16,2432]{1,0:T(8,128)(2,1)S(1)}, u32[]{:S(2)}, u32[]{:S(2)}) collective-permute-start(bf16[16,2432]{1,0:T(8,128)(2,1)S(1)} %collective-permute-done), channel_id=1, source_target_pairs={{0,3},{1,2},{2,1},{3,0},{4,7},{5,6},{6,5},{7,4},{8,11},{9,10},{10,... | collective-permute-start | bytes 233480 | tf_op jit(solution)/shard_map/ppermute | solution.py:20
  10.7 4.6 %collective-permute-done.1 = bf16[16,2432]{1,0:T(8,128)(2,1)S(1)} collective-permute-done((bf16[16,2432]{1,0:T(8,128)(2,1)S(1)}, bf16[16,2432]{1,0:T(8,128)(2,1)S(1)}, u32[]{:S(2)}, u32[]{:S(2)}) %collective-permute-start.1) | collective-permute-done | bytes 77856 | tf_op jit(solution)/shard_map/ppermute | solution.py:20
  15.4 1.7 %collective-permute-start.6 = (bf16[16,2432]{1,0:T(8,128)(2,1)S(1)}, bf16[16,2432]{1,0:T(8,128)(2,1)S(1)}, u32[]{:S(2)}, u32[]{:S(2)}) collective-permute-start(bf16[16,2432]{1,0:T(8,128)(2,1)S(1)} %collective-permute-done.2), channel_id=1, source_target_pairs={{0,3},{1,2},{2,1},{3,0},{4,7},{5,6},{6,5},{7,4},{8,11},{9,10},{10,... | collective-permute-start | bytes 233480 | tf_op jit(solution)/shard_map/ppermute | solution.py:20
  17.3 2.7 %collective-permute-done.5 = bf16[16,2432]{1,0:T(8,128)(2,1)S(1)} collective-permute-done((bf16[16,2432]{1,0:T(8,128)(2,1)S(1)}, bf16[16,2432]{1,0:T(8,128)(2,1)S(1)}, u32[]{:S(2)}, u32[]{:S(2)}) %collective-permute-start.5) | collective-permute-done | bytes 77856 | tf_op jit(solution)/shard_map/ppermute | solution.py:20
  20.0 1.5 %collective-permute-done.6 = bf16[16,2432]{1,0:T(8,128)(2,1)S(1)} collective-permute-done((bf16[16,2432]{1,0:T(8,128)(2,1)S(1)}, bf16[16,2432]{1,0:T(8,128)(2,1)S(1)}, u32[]{:S(2)}, u32[]{:S(2)}) %collective-permute-start.6) | collective-permute-done | bytes 77856 | tf_op jit(solution)/shard_map/ppermute | solution.py:20
  21.5 0.2 collective-permute-start.7
  21.7 1.9 %collective-permute-done.7 = bf16[8,16,2432]{2,1,0:T(8,128)(2,1)S(1)} collective-permute-done((bf16[8,16,2432]{2,1,0:T(8,128)(2,1)S(1)}, bf16[8,16,2432]{2,1,0:T(8,128)(2,1)S(1)}, u32[]{:S(2)}, u32[]{:S(2)}) %collective-permute-start.7) | collective-permute-done | bytes 622624 | tf_op jit(solution)/shard_map/ppermute | solution.py:20
  23.7 3.8 %fusion.11 = (f32[256]{0:T(256)S(1)}, f32[256,1024]{1,0:T(8,128)S(1)}) fusion(bf16[2304,1024]{1,0:T(8,128)(2,1)} %param.8, bf16[256,2432]{1,0:T(8,128)(2,1)S(1)} %bitcast.49), kind=kOutput, calls=%fused_computation.55 | convolution fusion | flops 1208483584 | bytes 6947840 | tf_op jit(solution)/shard_map/dot_general | solution.py:50
  27.5 0.1 copy.20
  27.6 0.1 stack.66
  27.7 0.5 %fusion.1 = (f32[256]{0:T(256)S(1)}, f32[256]{0:T(256)S(1)}, f32[256]{0:T(256)S(1)}) fusion(f32[256,1024]{1,0:T(8,128)S(1)} %get-tuple-element.32, f32[256]{0:T(256)S(1)} %get-tuple-element.31, s32[256]{0:T(256)S(1)} %bitcast.50), kind=kLoop, calls=%fused_computation.6 | loop fusion | flops 1834240 | bytes 1053696 | tf_op jit(solution)/shard_map/reduce_sum | solution.py:53
  28.3 0.1 stack.68
  28.5 0.8 %select_reduce_fusion.1 = f32[16,4,16]{2,1,0:T(4,128)} fusion(f32[16,4,16]{2,0,1:T(8,128)S(1)} %maximum_bitcast_fusion, pred[16,16]{1,0:T(8,128)(4,1)S(1)} %iota_compare_fusion.2), kind=kLoop, calls=%fused_computation.7 | loop fusion | flops 31744 | bytes 8448 | tf_op jit(solution)/shard_map/reduce_sum | solution.py:61
  29.3 4.7 %all-to-all-start = ((f32[16,4,16]{2,1,0:T(4,128)}), f32[16,4,16]{2,1,0:T(4,128)S(1)}, u32[]{:S(2)}, u32[]{:S(2)}) async-start(f32[16,4,16]{2,1,0:T(4,128)} %select_reduce_fusion.1), calls=%async_computation | async-start | bytes 65536 | tf_op jit(solution)/shard_map/all_to_all | solution.py:62
  34.7 6.0 %all-to-all-done = f32[16,4,16]{2,1,0:T(4,128)S(1)} async-done(((f32[16,4,16]{2,1,0:T(4,128)}), f32[16,4,16]{2,1,0:T(4,128)S(1)}, u32[]{:S(2)}, u32[]{:S(2)}) %all-to-all-start) | async-done | bytes 4128 | tf_op jit(solution)/shard_map/all_to_all | solution.py:62
  40.8 0.5 %compare_select_fusion.3 = (f32[16]{0:T(128)}, f32[16]{0:T(128)}) fusion(f32[16]{0:T(128)S(1)} %get-tuple-element.5, f32[16]{0:T(128)S(1)} %get-tuple-element.6, f32[16]{0:T(128)S(1)} %reduce_max.19, s32[]{:T(128)} %bitcast.42, f32[16]{0:T(128)S(1)} %reduce_sum.77), kind=kLoop, calls=%fused_computation.43 | loop fusion | flops 128 | bytes 388 | tf_op jit(solution)/shard_map/jit(_where)/select_n | solution.py:72
  (31 shorter events, 0.6 us)
Async XLA Ops:
  0.6 21.0 %copy-start = (s32[16]{0:T(128)S(1)}, s32[16]{0:T(128)}, u32[]{:S(2)}) copy-start(s32[16]{0:T(128)} %constant.51.clone) | copy-start | bytes 196
  3.4 6.8 %collective-permute-start = (bf16[16,2432]{1,0:T(8,128)(2,1)S(1)}, bf16[16,2432]{1,0:T(8,128)(2,1)S(1)}, u32[]{:S(2)}, u32[]{:S(2)}) collective-permute-start(bf16[16,2432]{1,0:T(8,128)(2,1)S(1)} %fusion.6), channel_id=1, source_target_pairs={{0,5},{1,4},{2,7},{3,6},{4,1},{5,0},{6,3},{7,2},{8,13},{9,12},{10,... | collective-permute-start | bytes 233480 | tf_op jit(solution)/shard_map/ppermute | solution.py:20
  6.0 9.4 %collective-permute-start.1 = (bf16[16,2432]{1,0:T(8,128)(2,1)S(1)}, bf16[16,2432]{1,0:T(8,128)(2,1)S(1)}, u32[]{:S(2)}, u32[]{:S(2)}) collective-permute-start(bf16[16,2432]{1,0:T(8,128)(2,1)S(1)} %fusion.6), channel_id=1, source_target_pairs={{0,8},{1,9},{2,10},{3,11},{4,12},{5,13},{6,14},{7,15},{8,0},{9,1},... | collective-permute-start | bytes 233480 | tf_op jit(solution)/shard_map/ppermute | solution.py:20
  8.6 6.8 %collective-permute-start.2 = (bf16[16,2432]{1,0:T(8,128)(2,1)S(1)}, bf16[16,2432]{1,0:T(8,128)(2,1)S(1)}, u32[]{:S(2)}, u32[]{:S(2)}) collective-permute-start(bf16[16,2432]{1,0:T(8,128)(2,1)S(1)} %fusion.6), channel_id=1, source_target_pairs={{0,13},{1,12},{2,15},{3,14},{4,9},{5,8},{6,11},{7,10},{8,5},{9,4},... | collective-permute-start | bytes 233480 | tf_op jit(solution)/shard_map/ppermute | solution.py:20
  8.7 8.4 %collective-permute-start.3 = (bf16[16,2432]{1,0:T(8,128)(2,1)S(1)}, bf16[16,2432]{1,0:T(8,128)(2,1)S(1)}, u32[]{:S(2)}, u32[]{:S(2)}) collective-permute-start(bf16[16,2432]{1,0:T(8,128)(2,1)S(1)} %fusion.6), channel_id=1, source_target_pairs={{0,3},{1,2},{2,1},{3,0},{4,7},{5,6},{6,5},{7,4},{8,11},{9,10},{10,... | collective-permute-start | bytes 233480 | tf_op jit(solution)/shard_map/ppermute | solution.py:20
  10.2 7.0 %collective-permute-start.4 = (bf16[16,2432]{1,0:T(8,128)(2,1)S(1)}, bf16[16,2432]{1,0:T(8,128)(2,1)S(1)}, u32[]{:S(2)}, u32[]{:S(2)}) collective-permute-start(bf16[16,2432]{1,0:T(8,128)(2,1)S(1)} %collective-permute-done), channel_id=1, source_target_pairs={{0,3},{1,2},{2,1},{3,0},{4,7},{5,6},{6,5},{7,4},{8,11},{9,10},{10,... | collective-permute-start | bytes 233480 | tf_op jit(solution)/shard_map/ppermute | solution.py:20
  15.4 4.6 %collective-permute-start.5 = (bf16[16,2432]{1,0:T(8,128)(2,1)S(1)}, bf16[16,2432]{1,0:T(8,128)(2,1)S(1)}, u32[]{:S(2)}, u32[]{:S(2)}) collective-permute-start(bf16[16,2432]{1,0:T(8,128)(2,1)S(1)} %collective-permute-done.1), channel_id=1, source_target_pairs={{0,3},{1,2},{2,1},{3,0},{4,7},{5,6},{6,5},{7,4},{8,11},{9,10},{10,... | collective-permute-start | bytes 233480 | tf_op jit(solution)/shard_map/ppermute | solution.py:20
  15.4 6.1 %collective-permute-start.6 = (bf16[16,2432]{1,0:T(8,128)(2,1)S(1)}, bf16[16,2432]{1,0:T(8,128)(2,1)S(1)}, u32[]{:S(2)}, u32[]{:S(2)}) collective-permute-start(bf16[16,2432]{1,0:T(8,128)(2,1)S(1)} %collective-permute-done.2), channel_id=1, source_target_pairs={{0,3},{1,2},{2,1},{3,0},{4,7},{5,6},{6,5},{7,4},{8,11},{9,10},{10,... | collective-permute-start | bytes 233480 | tf_op jit(solution)/shard_map/ppermute | solution.py:20
  21.5 2.1 %collective-permute-start.7 = (bf16[8,16,2432]{2,1,0:T(8,128)(2,1)S(1)}, bf16[8,16,2432]{2,1,0:T(8,128)(2,1)S(1)}, u32[]{:S(2)}, u32[]{:S(2)}) collective-permute-start(bf16[8,16,2432]{2,1,0:T(8,128)(2,1)S(1)} %get-tuple-element.7), channel_id=1, source_target_pairs={{0,1},{1,0},{2,3},{3,2},{4,5},{5,4},{6,7},{7,6},{8,9},{9,8},{10,11... | collective-permute-start | bytes 1867784 | tf_op jit(solution)/shard_map/ppermute | solution.py:20
  29.3 11.4 %all-to-all-start = ((f32[16,4,16]{2,1,0:T(4,128)}), f32[16,4,16]{2,1,0:T(4,128)S(1)}, u32[]{:S(2)}, u32[]{:S(2)}) async-start(f32[16,4,16]{2,1,0:T(4,128)} %select_reduce_fusion.1), calls=%async_computation | async-start | bytes 65536 | tf_op jit(solution)/shard_map/all_to_all | solution.py:62

commit v2 on v1

v2 whole, which is shorter than its diff:
```python
import functools

import jax
import jax.numpy as jnp
from jax import lax
from jax.experimental import pallas as pl
from jax.experimental.pallas import tpu as pltpu
from jax.sharding import PartitionSpec as P

logit_scale = 256.0 / 2304.0
CAP = 10
HEAD = 8
TAIL = CAP - HEAD
LANES = 128
PER_TILE = HEAD // TAIL


def gather_masks(n):
    if n == 16:
        return [[5, 8, 13], [3], [1]]
    steps, bit = [], n // 2
    while bit:
        steps.append([bit])
        bit //= 2
    return steps


def swap(block, mask, n):
    return lax.ppermute(block, "vocab", [(i, i ^ mask) for i in range(n)])


def strip_at(chunks, c):
    tile, place = divmod(c, PER_TILE)
    return slice(TAIL * place, TAIL * place + TAIL), slice((chunks + tile) * LANES, (chunks + tile + 1) * LANES)


def front_kernel(hidden_ref, gain_ref, targets_ref, block_ref):
    slots, width = hidden_ref.shape
    chunks = width // LANES
    values = hidden_ref[...].astype(jnp.float32)
    square_mean = jnp.sum(values * values, axis=1, keepdims=True) * (1.0 / width)
    gain = gain_ref[...].reshape(1, width)
    normed = (values * lax.rsqrt(square_mean + 1e-05) * gain).astype(jnp.bfloat16)
    block_ref[:, :width] = normed[:HEAD]
    for c in range(chunks):
        rows, columns = strip_at(chunks, c)
        block_ref[rows, columns] = normed[HEAD:CAP, c * LANES:(c + 1) * LANES]
    ids = jnp.broadcast_to(targets_ref[...].reshape(1, slots), (TAIL, slots))
    part = lax.broadcasted_iota(jnp.int32, ids.shape, 0)
    ids = jnp.where(part == 0, lax.shift_right_logical(ids, 8), ids & 255)
    rows, columns = strip_at(chunks, chunks)
    block_ref[rows, columns.start:columns.start + slots] = ids.astype(jnp.float32).astype(jnp.bfloat16)


def front(hidden, gain, targets):
    chunks = hidden.shape[1] // LANES
    tiles = chunks + -(-(chunks + 1) // PER_TILE)
    return pl.pallas_call(
        front_kernel,
        out_shape=jax.ShapeDtypeStruct((HEAD, tiles * LANES), jnp.bfloat16),
        in_specs=[pl.BlockSpec(memory_space=pltpu.VMEM)] * 3,
        out_specs=pl.BlockSpec(memory_space=pltpu.VMEM),
        name="norm_and_pack",
    )(hidden, gain, targets)


def stats_kernel(owners, n_cols, near_ref, far_ref, weight_ref, out_ref, rows_ref, logits_ref):
    n = len(owners)
    half = n // 2
    width, vocab_dev = weight_ref.shape
    chunks = width // LANES
    me = lax.axis_index("vocab")
    start = me * vocab_dev
    base = n * HEAD
    lane = lax.broadcasted_iota(jnp.int32, (HEAD, LANES), 1)
    sub = lax.broadcasted_iota(jnp.int32, (HEAD, LANES), 0)
    id_rows, id_columns = strip_at(chunks, chunks)
    head_ids, tail_ids = [], []
    for b in range(n):
        ref, at = (near_ref, b) if b < half else (far_ref, b - half)
        rows_ref[b * HEAD:(b + 1) * HEAD, :] = ref[at, :, :width]
        for c in range(chunks):
            r, k = strip_at(chunks, c)
            rows_ref[base + TAIL * b:base + TAIL * (b + 1), c * LANES:(c + 1) * LANES] = ref[at, r, k]
        ids = ref[at, id_rows, id_columns].astype(jnp.float32)
        ids = ids[0:1] * 256.0 + ids[1:2]
        ids = jnp.broadcast_to(ids, (HEAD, LANES))
        head_ids.append(jnp.sum(jnp.where(lane == sub, ids, 0.0), axis=1, keepdims=True))
        tail_ids.append(jnp.sum(jnp.where((lane == sub + HEAD)[:TAIL], ids[:TAIL], 0.0), axis=1, keepdims=True))
    wanted = jnp.concatenate(head_ids + tail_ids, axis=0).astype(jnp.int32) - start
    m = n * CAP
    peak = None
    for j in range(0, vocab_dev, n_cols):
        z = jnp.dot(rows_ref[...], weight_ref[:, j:j + n_cols], preferred_element_type=jnp.float32) * logit_scale
        logits_ref[:, j:j + n_cols] = z
        top = z[:, :LANES]
        for k in range(LANES, n_cols, LANES):
            top = jnp.maximum(top, z[:, k:k + LANES])
        peak = top if peak is None else jnp.maximum(peak, top)
    peak = jnp.max(peak, axis=1, keepdims=True)
    total = jnp.zeros((m, LANES), jnp.float32)
    moment = jnp.zeros((m, LANES), jnp.float32)
    chosen = jnp.zeros((m, LANES), jnp.float32)
    column = lax.broadcasted_iota(jnp.int32, (m, LANES), 1)
    for j in range(0, vocab_dev, LANES):
        z = logits_ref[:, j:j + LANES]
        e = jnp.exp(z - peak)
        total += e
        moment += e * z
        chosen += jnp.where(column == wanted - j, z, 0.0)
    total = jnp.sum(total, axis=1, keepdims=True)
    moment = jnp.sum(moment, axis=1, keepdims=True)
    chosen = jnp.sum(chosen, axis=1, keepdims=True)
    table = jnp.where(column == 0, peak, jnp.where(column == 1, total, jnp.where(column == 2, moment, chosen)))
    for b in range(n):
        to = me ^ owners[b]
        out_ref[to, :HEAD] = table[b * HEAD:(b + 1) * HEAD]
        out_ref[to, HEAD:CAP] = table[base + TAIL * b:base + TAIL * (b + 1)]


def row_stats(owners, near, far, weight):
    n = len(owners)
    width, vocab_dev = weight.shape
    return pl.pallas_call(
        functools.partial(stats_kernel, owners, 256),
        out_shape=jax.ShapeDtypeStruct((n, 16, LANES), jnp.float32),
        in_specs=[pl.BlockSpec(memory_space=pltpu.VMEM)] * 3,
        out_specs=pl.BlockSpec(memory_space=pltpu.VMEM),
        scratch_shapes=[
            pltpu.VMEM((n * CAP, width), jnp.bfloat16),
            pltpu.VMEM((n * CAP, vocab_dev), jnp.float32),
        ],
        compiler_params=pltpu.CompilerParams(vmem_limit_bytes=32 * 1024 * 1024),
        name="row_stats",
    )(near, far, weight)


def on_device(n, hidden, norm_gain, head_weight, targets, counts):
    slots = hidden.shape[0]
    block = front(hidden, norm_gain, targets)
    blocks, owners = [block], [0]
    *steps, last = gather_masks(n)
    for masks in steps:
        got = [swap(b, mask, n) for mask in masks for b in blocks]
        owners = owners + [o ^ mask for mask in masks for o in owners]
        blocks = blocks + got
    near = jnp.stack(blocks)
    far = swap(near, last[0], n)
    owners = owners + [o ^ last[0] for o in owners]
    stats = row_stats(tuple(owners), near, far, head_weight)
    back = lax.all_to_all(stats, "vocab", 0, 0, tiled=True)
    peaks, totals, moments, chosens = (back[:, :slots, k] for k in range(4))
    scored = jnp.arange(slots, dtype=jnp.int32) < counts[0]
    peak = jnp.max(peaks, axis=0)
    factor = jnp.exp(peaks - peak[None])
    total = jnp.sum(totals * factor, axis=0)
    moment = jnp.sum(moments * factor, axis=0)
    chosen = jnp.sum(chosens, axis=0)
    log_total = jnp.log(total)
    logprob = jnp.where(scored, chosen - peak - log_total, jnp.float32(0.0))
    entropy = jnp.where(scored, peak + log_total - moment / total, jnp.float32(0.0))
    return (logprob, entropy)


def solution(mesh):
    n = mesh.shape["vocab"]
    in_specs = (
        P(("req", "vocab"), None),
        P(),
        P(None, "vocab"),
        P(("req", "vocab")),
        P(("req", "vocab")),
    )
    out_specs = (P(("req", "vocab")), P(("req", "vocab")))

    def step(*args):
        return on_device(n, *args)

    return jax.shard_map(step, mesh=mesh, in_specs=in_specs, out_specs=out_specs, check_vma=False)
```

time: 41.6 us -> 36.6 us (0.88)
  waiting for transfers between devices: 16.8 us -> 12.9 us
  matrix products: 3.81 us -> 0 us
  other arithmetic: 4.69 us -> 1.02 us
  Pallas kernels: 0 us -> 3.51 us
  local copies, waits for them, and re-layouts: 0.73 us -> 3.24 us
    ppermute x8, waiting for transfers between devices: 10.8 us -> 5.59 us  [swap(): return lax.ppermute(block, 'vocab', [(i, i ^ mask) for i in range(n)])]
    dot_general x1 -> x0, matrix products: 3.81 us -> none  [on_device(): jnp.dot(gathered, head_weight, preferred_element_type=jnp.float32)]
    pallas_call x0 -> x2, Pallas kernels: none -> 3.51 us  [the longest x1 1.87 us: row_stats(): pl.pallas_call(functools.partial(stats_kernel, owners, 256), out_shape=ja...]
    unnamed x10 -> x9, local copies, waits for them, and re-layouts: 0.31 us -> 3.23 us
    reduce_sum x4 -> x0, other arithmetic: 2.38 us -> none  [the longest x1 1.02 us: on_device(): square_mean = jnp.mean(values * values, axis=1, keepdims=True)]
    all_to_all x1, waiting for transfers between devices: 5.99 us -> 7.29 us  [on_device(): back = lax.all_to_all(stats, 'vocab', 0, 0, tiled=True)]
    convert_element_type x2 -> x0, other arithmetic: 0.99 us -> none  [the longest x1 0.98 us: on_device(): (values * lax.rsqrt(square_mean + 1e-05) * norm_gain[None, :]).astype(jnp...]
    another operation x2 -> x0, other arithmetic: 0.68 us -> none  [on_device(): jnp.stack([targets // 256, targets % 256], axis=1).astype(jnp.bfloat16)]
  transfers between devices with their start and end apart: 9 -> 9, of which waited for: 5 -> 6; matrix products, arithmetic and copies ran while one was open for 0% -> 2% of each run, Pallas kernels for 0% -> 0%
where the time goes in v2:
time: 36.6 us; the launch traced here: 36.3 us
  starting transfers between devices  14.3 us (39%)
  waiting for transfers between devices  12.9 us (35%)
  Pallas kernels  3.51 us (10%)
  local copies, waits for them, and re-layouts  3.24 us (9%)
  between operations  1.32 us (4%)
  other arithmetic  1.02 us (3%)
    ppermute x8, starting transfers between devices, swap(): return lax.ppermute(block, 'vocab', [(i, i ^ mask) for i in range(n)])  9.31 us
    all_to_all x1, waiting for transfers between devices, on_device(): back = lax.all_to_all(stats, 'vocab', 0, 0, tiled=True)  7.29 us
    ppermute x8, waiting for transfers between devices, swap(): return lax.ppermute(block, 'vocab', [(i, i ^ mask) for i in range(n)])  5.59 us
    all_to_all x1, starting transfers between devices, on_device(): back = lax.all_to_all(stats, 'vocab', 0, 0, tiled=True)  5.03 us
    unnamed x9, local copies, waits for them, and re-layouts  3.23 us
    pallas_call x1, Pallas kernels, row_stats(): pl.pallas_call(functools.partial(stats_kernel, owners, 256), out_shape=ja...  1.87 us
    pallas_call x1, Pallas kernels, front(): pl.pallas_call(front_kernel, out_shape=jax.ShapeDtypeStruct((HEAD, tiles...  1.64 us
  transfers between devices with their start and end apart: 9, of which 6 were waited for; matrix products, arithmetic and copies ran while one was open for 2% of the time, Pallas kernels for 0%

profile of v2, /device:TPU:0, one launch (start us, length us, event | category | flops | bytes accessed | tf_op | source)
XLA Modules:
  0.0 36.3 jit_solution(14072159303703609882)
XLA Ops:
  0.6 1.6 %norm_and_pack.1 = bf16[8,2944]{1,0:T(8,128)(2,1)} custom-call(bf16[16,2304]{1,0:T(8,128)(2,1)} %hidden_ref.1, f32[2304]{0:T(1024)} %gain_ref.1, s32[16]{0:T(128)} %targets_ref.1), custom_call_target="tpu_custom_call" | custom-call | tf_op jit(solution)/shard_map/norm_and_pack/pallas_call | solution.py:58
  2.3 2.5 %collective-permute-start = (bf16[8,2944]{1,0:T(8,128)(2,1)}, bf16[8,2944]{1,0:T(8,128)(2,1)S(1)}, u32[]{:S(2)}, u32[]{:S(2)}) collective-permute-start(bf16[8,2944]{1,0:T(8,128)(2,1)} %norm_and_pack.1), channel_id=1, source_target_pairs={{0,5},{1,4},{2,7},{3,6},{4,1},{5,0},{6,3},{7,2},{8,13},{9,12},{10,... | collective-permute-start | bytes 141320 | tf_op jit(solution)/shard_map/ppermute | solution.py:29
  4.7 2.6 %collective-permute-start.1 = (bf16[8,2944]{1,0:T(8,128)(2,1)}, bf16[8,2944]{1,0:T(8,128)(2,1)S(1)}, u32[]{:S(2)}, u32[]{:S(2)}) collective-permute-start(bf16[8,2944]{1,0:T(8,128)(2,1)} %norm_and_pack.1), channel_id=1, source_target_pairs={{0,8},{1,9},{2,10},{3,11},{4,12},{5,13},{6,14},{7,15},{8,0},{9,1},... | collective-permute-start | bytes 141320 | tf_op jit(solution)/shard_map/ppermute | solution.py:29
  7.3 0.2 collective-permute-start.2
  7.5 1.4 %collective-permute-start.3 = (bf16[8,2944]{1,0:T(8,128)(2,1)}, bf16[8,2944]{1,0:T(8,128)(2,1)S(1)}, u32[]{:S(2)}, u32[]{:S(2)}) collective-permute-start(bf16[8,2944]{1,0:T(8,128)(2,1)} %norm_and_pack.1), channel_id=1, source_target_pairs={{0,3},{1,2},{2,1},{3,0},{4,7},{5,6},{6,5},{7,4},{8,11},{9,10},{10,... | collective-permute-start | bytes 141320 | tf_op jit(solution)/shard_map/ppermute | solution.py:29
  8.9 0.8 %bitcast_dynamic-update-slice_fusion.7 = bf16[8,8,2944]{2,1,0:T(8,128)(2,1)S(1)} fusion(bf16[8,2944]{1,0:T(8,128)(2,1)} %norm_and_pack.1), kind=kLoop, calls=%fused_computation.12 | loop fusion | bytes 94208
  9.7 0.0 collective-permute-done
  9.7 0.3 collective-permute-start.4
  10.1 1.1 %collective-permute-done.1 = bf16[8,2944]{1,0:T(8,128)(2,1)S(1)} collective-permute-done((bf16[8,2944]{1,0:T(8,128)(2,1)}, bf16[8,2944]{1,0:T(8,128)(2,1)S(1)}, u32[]{:S(2)}, u32[]{:S(2)}) %collective-permute-start.1) | collective-permute-done | bytes 47136 | tf_op jit(solution)/shard_map/ppermute | solution.py:29
  11.2 0.3 collective-permute-start.5
  11.6 1.3 %collective-permute-done.2 = bf16[8,2944]{1,0:T(8,128)(2,1)S(1)} collective-permute-done((bf16[8,2944]{1,0:T(8,128)(2,1)}, bf16[8,2944]{1,0:T(8,128)(2,1)S(1)}, u32[]{:S(2)}, u32[]{:S(2)}) %collective-permute-start.2) | collective-permute-done | bytes 47136 | tf_op jit(solution)/shard_map/ppermute | solution.py:29
  12.8 1.6 %collective-permute-start.6 = (bf16[8,2944]{1,0:T(8,128)(2,1)S(1)}, bf16[8,2944]{1,0:T(8,128)(2,1)S(1)}, u32[]{:S(2)}, u32[]{:S(2)}) collective-permute-start(bf16[8,2944]{1,0:T(8,128)(2,1)S(1)} %collective-permute-done.2), channel_id=1, source_target_pairs={{0,3},{1,2},{2,1},{3,0},{4,7},{5,6},{6,5},{7,4},{8,11},{9,10},{10,... | collective-permute-start | bytes 141320 | tf_op jit(solution)/shard_map/ppermute | solution.py:29
  14.4 0.0 collective-permute-done.3
  14.4 0.0 collective-permute-done.4
  14.4 0.7 %collective-permute-done.5 = bf16[8,2944]{1,0:T(8,128)(2,1)S(1)} collective-permute-done((bf16[8,2944]{1,0:T(8,128)(2,1)S(1)}, bf16[8,2944]{1,0:T(8,128)(2,1)S(1)}, u32[]{:S(2)}, u32[]{:S(2)}) %collective-permute-start.5) | collective-permute-done | bytes 47136 | tf_op jit(solution)/shard_map/ppermute | solution.py:29
  15.2 1.2 %collective-permute-done.6 = bf16[8,2944]{1,0:T(8,128)(2,1)S(1)} collective-permute-done((bf16[8,2944]{1,0:T(8,128)(2,1)S(1)}, bf16[8,2944]{1,0:T(8,128)(2,1)S(1)}, u32[]{:S(2)}, u32[]{:S(2)}) %collective-permute-start.6) | collective-permute-done | bytes 47136 | tf_op jit(solution)/shard_map/ppermute | solution.py:29
  16.3 0.4 %collective-permute-start.7 = (bf16[8,8,2944]{2,1,0:T(8,128)(2,1)S(1)}, bf16[8,8,2944]{2,1,0:T(8,128)(2,1)S(1)}, u32[]{:S(2)}, u32[]{:S(2)}) collective-permute-start(bf16[8,8,2944]{2,1,0:T(8,128)(2,1)S(1)} %bitcast_dynamic-update-slice_fusion.near_ref), channel_id=1, source_target_pairs={{0,1},{1,0},{2,3},{3,2},{4,5},{5,4},{6,7},{7,6},{8,9},{9,8},{10,11... | collective-permute-start | bytes 1130504 | tf_op jit(solution)/shard_map/ppermute | solution.py:29
  16.8 1.3 %collective-permute-done.7.far_ref = bf16[8,8,2944]{2,1,0:T(8,128)(2,1)S(1)} collective-permute-done((bf16[8,8,2944]{2,1,0:T(8,128)(2,1)S(1)}, bf16[8,8,2944]{2,1,0:T(8,128)(2,1)S(1)}, u32[]{:S(2)}, u32[]{:S(2)}) %collective-permute-start.7) | collective-permute-done | bytes 376864 | tf_op jit(solution)/shard_map/ppermute | solution.py:29
  18.1 2.3 %copy-done = bf16[2304,1024]{1,0:T(8,128)(2,1)S(1)} copy-done((bf16[2304,1024]{1,0:T(8,128)(2,1)S(1)}, bf16[2304,1024]{1,0:T(8,128)(2,1)}, u32[]{:S(2)}) %copy-start) | copy-done | bytes 4718616
  20.4 1.9 %row_stats.1 = f32[16,16,128]{2,1,0:T(8,128)} custom-call(bf16[8,8,2944]{2,1,0:T(8,128)(2,1)S(1)} %bitcast_dynamic-update-slice_fusion.near_ref, bf16[8,8,2944]{2,1,0:T(8,128)(2,1)S(1)} %collective-permute-done.7.far_ref, bf16[2304,1024]{1,0:T(8,128)(2,1)S(1)} %copy-done), custom_call_target="tpu_custom_call" | custom-call | tf_op jit(solution)/shard_map/row_stats/pallas_call | solution.py:124
  22.3 5.0 %all-to-all-start = ((f32[16,16,128]{2,1,0:T(8,128)}), f32[16,16,128]{2,1,0:T(8,128)S(1)}, u32[]{:S(2)}, u32[]{:S(2)}) async-start(f32[16,16,128]{2,1,0:T(8,128)} %row_stats.1), calls=%async_computation | async-start | bytes 262144 | tf_op jit(solution)/shard_map/all_to_all | solution.py:151
  28.0 7.3 %all-to-all-done = f32[16,16,128]{2,1,0:T(8,128)S(1)} async-done(((f32[16,16,128]{2,1,0:T(8,128)}), f32[16,16,128]{2,1,0:T(8,128)S(1)}, u32[]{:S(2)}, u32[]{:S(2)}) %all-to-all-start) | async-done | bytes 131104 | tf_op jit(solution)/shard_map/all_to_all | solution.py:151
  35.3 0.5 %slice_reduce_fusion = (f32[16,16]{1,0:T(8,128)S(1)}, f32[16,16]{1,0:T(8,128)S(1)}, f32[16,16]{1,0:T(8,128)S(1)}, f32[16]{0:T(128)S(1)}, f32[16]{0:T(128)S(1)}) fusion(f32[16,16,128]{2,1,0:T(8,128)S(1)} %all-to-all-done), kind=kLoop, calls=%fused_computation | loop fusion | flops 480 | bytes 7296 | tf_op jit(solution)/shard_map/slice | solution.py:152
  35.8 0.5 %compare_select_fusion = (f32[16]{0:T(128)}, f32[16]{0:T(128)}) fusion(f32[16]{0:T(128)S(1)} %get-tuple-element.7, f32[16]{0:T(128)S(1)} %get-tuple-element.8, f32[16]{0:T(128)S(1)} %get-tuple-element.5, s32[]{:T(128)} %bitcast.17, f32[16]{0:T(128)S(1)} %get-tuple-element.6), kind=kLoop, calls=%fused_computation.16 | loop fusion | flops 128 | bytes 388 | tf_op jit(solution)/shard_map/jit(_where)/select_n | solution.py:161
  (9 shorter events, 0.1 us)
Async XLA Ops:
  2.3 7.5 %collective-permute-start = (bf16[8,2944]{1,0:T(8,128)(2,1)}, bf16[8,2944]{1,0:T(8,128)(2,1)S(1)}, u32[]{:S(2)}, u32[]{:S(2)}) collective-permute-start(bf16[8,2944]{1,0:T(8,128)(2,1)} %norm_and_pack.1), channel_id=1, source_target_pairs={{0,5},{1,4},{2,7},{3,6},{4,1},{5,0},{6,3},{7,2},{8,13},{9,12},{10,... | collective-permute-start | bytes 141320 | tf_op jit(solution)/shard_map/ppermute | solution.py:29
  4.7 6.5 %collective-permute-start.1 = (bf16[8,2944]{1,0:T(8,128)(2,1)}, bf16[8,2944]{1,0:T(8,128)(2,1)S(1)}, u32[]{:S(2)}, u32[]{:S(2)}) collective-permute-start(bf16[8,2944]{1,0:T(8,128)(2,1)} %norm_and_pack.1), channel_id=1, source_target_pairs={{0,8},{1,9},{2,10},{3,11},{4,12},{5,13},{6,14},{7,15},{8,0},{9,1},... | collective-permute-start | bytes 141320 | tf_op jit(solution)/shard_map/ppermute | solution.py:29
  7.3 5.5 %collective-permute-start.2 = (bf16[8,2944]{1,0:T(8,128)(2,1)}, bf16[8,2944]{1,0:T(8,128)(2,1)S(1)}, u32[]{:S(2)}, u32[]{:S(2)}) collective-permute-start(bf16[8,2944]{1,0:T(8,128)(2,1)} %norm_and_pack.1), channel_id=1, source_target_pairs={{0,13},{1,12},{2,15},{3,14},{4,9},{5,8},{6,11},{7,10},{8,5},{9,4},... | collective-permute-start | bytes 141320 | tf_op jit(solution)/shard_map/ppermute | solution.py:29
  7.5 6.9 %collective-permute-start.3 = (bf16[8,2944]{1,0:T(8,128)(2,1)}, bf16[8,2944]{1,0:T(8,128)(2,1)S(1)}, u32[]{:S(2)}, u32[]{:S(2)}) collective-permute-start(bf16[8,2944]{1,0:T(8,128)(2,1)} %norm_and_pack.1), channel_id=1, source_target_pairs={{0,3},{1,2},{2,1},{3,0},{4,7},{5,6},{6,5},{7,4},{8,11},{9,10},{10,... | collective-permute-start | bytes 141320 | tf_op jit(solution)/shard_map/ppermute | solution.py:29
  9.7 4.7 %collective-permute-start.4 = (bf16[8,2944]{1,0:T(8,128)(2,1)S(1)}, bf16[8,2944]{1,0:T(8,128)(2,1)S(1)}, u32[]{:S(2)}, u32[]{:S(2)}) collective-permute-start(bf16[8,2944]{1,0:T(8,128)(2,1)S(1)} %collective-permute-done), channel_id=1, source_target_pairs={{0,3},{1,2},{2,1},{3,0},{4,7},{5,6},{6,5},{7,4},{8,11},{9,10},{10,... | collective-permute-start | bytes 141320 | tf_op jit(solution)/shard_map/ppermute | solution.py:29
  11.2 3.9 %collective-permute-start.5 = (bf16[8,2944]{1,0:T(8,128)(2,1)S(1)}, bf16[8,2944]{1,0:T(8,128)(2,1)S(1)}, u32[]{:S(2)}, u32[]{:S(2)}) collective-permute-start(bf16[8,2944]{1,0:T(8,128)(2,1)S(1)} %collective-permute-done.1), channel_id=1, source_target_pairs={{0,3},{1,2},{2,1},{3,0},{4,7},{5,6},{6,5},{7,4},{8,11},{9,10},{10,... | collective-permute-start | bytes 141320 | tf_op jit(solution)/shard_map/ppermute | solution.py:29
  12.8 3.5 %collective-permute-start.6 = (bf16[8,2944]{1,0:T(8,128)(2,1)S(1)}, bf16[8,2944]{1,0:T(8,128)(2,1)S(1)}, u32[]{:S(2)}, u32[]{:S(2)}) collective-permute-start(bf16[8,2944]{1,0:T(8,128)(2,1)S(1)} %collective-permute-done.2), channel_id=1, source_target_pairs={{0,3},{1,2},{2,1},{3,0},{4,7},{5,6},{6,5},{7,4},{8,11},{9,10},{10,... | collective-permute-start | bytes 141320 | tf_op jit(solution)/shard_map/ppermute | solution.py:29
  16.3 1.8 %collective-permute-start.7 = (bf16[8,8,2944]{2,1,0:T(8,128)(2,1)S(1)}, bf16[8,8,2944]{2,1,0:T(8,128)(2,1)S(1)}, u32[]{:S(2)}, u32[]{:S(2)}) collective-permute-start(bf16[8,8,2944]{2,1,0:T(8,128)(2,1)S(1)} %bitcast_dynamic-update-slice_fusion.near_ref), channel_id=1, source_target_pairs={{0,1},{1,0},{2,3},{3,2},{4,5},{5,4},{6,7},{7,6},{8,9},{9,8},{10,11... | collective-permute-start | bytes 1130504 | tf_op jit(solution)/shard_map/ppermute | solution.py:29
  18.1 2.3 %copy-start = (bf16[2304,1024]{1,0:T(8,128)(2,1)S(1)}, bf16[2304,1024]{1,0:T(8,128)(2,1)}, u32[]{:S(2)}) copy-start(bf16[2304,1024]{1,0:T(8,128)(2,1)} %weight_ref.1) | copy-start | bytes 14155780
  22.3 13.0 %all-to-all-start = ((f32[16,16,128]{2,1,0:T(8,128)}), f32[16,16,128]{2,1,0:T(8,128)S(1)}, u32[]{:S(2)}, u32[]{:S(2)}) async-start(f32[16,16,128]{2,1,0:T(8,128)} %row_stats.1), calls=%async_computation | async-start | bytes 262144 | tf_op jit(solution)/shard_map/all_to_all | solution.py:151

commit v3 on v2

v3 whole, which is shorter than its diff:
```python
import functools

import jax
import jax.numpy as jnp
from jax import lax
from jax.experimental import pallas as pl
from jax.experimental.pallas import tpu as pltpu
from jax.sharding import PartitionSpec as P

logit_scale = 256.0 / 2304.0
CAP = 10
HEAD = 8
TAIL = CAP - HEAD
LANES = 128
PER_TILE = HEAD // TAIL
FIELD = 16
VMEM = pl.BlockSpec(memory_space=pltpu.VMEM)
ANY = pl.BlockSpec(memory_space=pl.ANY)
MIB = 1024 * 1024


def gather_masks(n):
    if n == 16:
        return [[8, 5, 13], [3], [1]]
    steps, bit = [], n // 2
    while bit:
        steps.append([bit])
        bit //= 2
    return steps


def swap(block, mask, n):
    return lax.ppermute(block, "vocab", [(i, i ^ mask) for i in range(n)])


def in_hbm(array):
    return pltpu.with_memory_space_constraint(array, pltpu.HBM)


def strip_at(chunks, c):
    tile, place = divmod(c, PER_TILE)
    return slice(TAIL * place, TAIL * place + TAIL), slice((chunks + tile) * LANES, (chunks + tile + 1) * LANES)


def front_kernel(
    hidden_hbm, gain_hbm, targets_hbm, counts_ref, block_ref, scored_ref, hidden_ref, gain_ref, targets_ref, sems
):
    copies = [
        pltpu.make_async_copy(source, target, sems.at[i])
        for i, (source, target) in enumerate(
            [(hidden_hbm, hidden_ref), (gain_hbm, gain_ref), (targets_hbm, targets_ref)]
        )
    ]
    for copy in copies:
        copy.start()
    for copy in copies:
        copy.wait()
    slots, width = hidden_ref.shape
    chunks = width // LANES + 1
    values = hidden_ref[...].astype(jnp.float32)
    square_mean = jnp.sum(values * values, axis=1, keepdims=True) * (1.0 / width)
    gain = gain_ref[...].reshape(1, width)
    normed = (values * lax.rsqrt(square_mean + 1e-05) * gain).astype(jnp.bfloat16)
    lane = lax.broadcasted_iota(jnp.int32, (slots, LANES), 1)
    sub = lax.broadcasted_iota(jnp.int32, (slots, LANES), 0)
    ids = jnp.broadcast_to(targets_ref[...].reshape(1, slots), (slots, slots))
    own = lax.broadcasted_iota(jnp.int32, (slots, slots), 0) == lax.broadcasted_iota(jnp.int32, (slots, slots), 1)
    ids = jnp.sum(jnp.where(own, ids, 0).astype(jnp.float32), axis=1, keepdims=True).astype(jnp.int32)
    ids = jnp.where(lane == 0, lax.shift_right_logical(ids, 8), jnp.where(lane == 1, ids & 255, 0))
    ids = ids.astype(jnp.float32).astype(jnp.bfloat16)
    block_ref[:, :width] = normed[:HEAD]
    block_ref[:, width:width + LANES] = ids[:HEAD]
    for c in range(chunks):
        rows, columns = strip_at(chunks, c)
        chunk = ids if c == chunks - 1 else normed[:, c * LANES:(c + 1) * LANES]
        block_ref[rows, columns] = chunk[HEAD:CAP]
    scored_ref[...] = (lane[:HEAD] < counts_ref[0]).astype(jnp.float32)


def front(hidden, gain, targets, counts):
    slots, width = hidden.shape
    chunks = width // LANES + 1
    tiles = chunks + -(-chunks // PER_TILE)
    return pl.pallas_call(
        front_kernel,
        out_shape=(pltpu.VMEM((HEAD, tiles * LANES), jnp.bfloat16), pltpu.VMEM((HEAD, LANES), jnp.float32)),
        in_specs=[ANY] * 3 + [pl.BlockSpec(memory_space=pltpu.SMEM)],
        out_specs=[VMEM] * 2,
        scratch_shapes=[
            pltpu.VMEM(hidden.shape, hidden.dtype),
            pltpu.VMEM(gain.shape, gain.dtype),
            pltpu.VMEM(targets.shape, targets.dtype),
            pltpu.SemaphoreType.DMA((3,)),
        ],
        compiler_params=pltpu.CompilerParams(vmem_limit_bytes=4 * MIB),
        name="norm_and_pack",
    )(in_hbm(hidden), in_hbm(gain), in_hbm(targets), counts)


def fetch_kernel(after_ref, weight_ref, out_ref, sems):
    del after_ref
    parts = sems.shape[0]
    rows = weight_ref.shape[0] // parts
    copies = [
        pltpu.make_async_copy(weight_ref.at[pl.ds(i * rows, rows)], out_ref.at[pl.ds(i * rows, rows)], sems.at[i])
        for i in range(parts)
    ]
    for copy in copies:
        copy.start()
    for copy in copies:
        copy.wait()


def fetch(after, weight):
    return pl.pallas_call(
        fetch_kernel,
        out_shape=pltpu.VMEM(weight.shape, weight.dtype),
        in_specs=[ANY] * 2,
        out_specs=VMEM,
        scratch_shapes=[pltpu.SemaphoreType.DMA((8,))],
        cost_estimate=pl.CostEstimate(flops=0, bytes_accessed=2 * weight.size, transcendentals=0),
        compiler_params=pltpu.CompilerParams(vmem_limit_bytes=MIB),
        name="fetch_weights",
    )(after, in_hbm(weight))


def unpack_kernel(*refs):
    *blocks, out_ref = refs
    base = len(blocks) * HEAD
    chunks = out_ref.shape[1] // LANES
    for b, ref in enumerate(blocks):
        out_ref[b * HEAD:(b + 1) * HEAD, :] = ref[:, :chunks * LANES]
        for c in range(chunks):
            rows, columns = strip_at(chunks, c)
            out_ref[base + TAIL * b:base + TAIL * (b + 1), c * LANES:(c + 1) * LANES] = ref[rows, columns]


def unpack(blocks, width):
    return pl.pallas_call(
        unpack_kernel,
        out_shape=pltpu.VMEM((len(blocks) * CAP, width + LANES), jnp.bfloat16),
        in_specs=[VMEM] * len(blocks),
        out_specs=VMEM,
        compiler_params=pltpu.CompilerParams(vmem_limit_bytes=4 * MIB),
        name="unpack",
    )(*blocks)


def stats_kernel(owners, n_cols, near_ref, far_ref, weight_ref, out_ref, logits_ref):
    n = len(owners)
    half = n // 2
    width, vocab_dev = weight_ref.shape
    m = n * CAP
    me = lax.axis_index("vocab")
    rows = jnp.concatenate([near_ref[:, :width], far_ref[:, :width]], axis=0)
    ids = jnp.concatenate([near_ref[:, width:], far_ref[:, width:]], axis=0).astype(jnp.float32)
    wanted = (ids[:, 0:1] * 256.0 + ids[:, 1:2]).astype(jnp.int32) - me * vocab_dev
    peak = None
    for j in range(0, vocab_dev, n_cols):
        z = jnp.dot(rows, weight_ref[:, j:j + n_cols], preferred_element_type=jnp.float32) * logit_scale
        logits_ref[:, j:j + n_cols] = z
        for k in range(0, n_cols, LANES):
            part = z[:, k:k + LANES]
            peak = part if peak is None else jnp.maximum(peak, part)
    peak = jnp.max(peak, axis=1, keepdims=True)
    total = jnp.zeros((m, LANES), jnp.float32)
    moment = jnp.zeros((m, LANES), jnp.float32)
    chosen = jnp.zeros((m, LANES), jnp.float32)
    column = lax.broadcasted_iota(jnp.int32, (m, LANES), 1)
    for j in range(0, vocab_dev, LANES):
        z = logits_ref[:, j:j + LANES]
        e = jnp.exp(z - peak)
        total += e
        moment += e * z
        chosen += jnp.where(column == wanted - j, z, 0.0)
    total = jnp.sum(total, axis=1, keepdims=True)
    moment = jnp.sum(moment, axis=1, keepdims=True)
    chosen = jnp.sum(chosen, axis=1, keepdims=True)
    field = lax.shift_right_logical(column, 4)
    table = jnp.where(field == 0, peak, jnp.where(field == 1, total, jnp.where(field == 2, moment, chosen)))
    lane = lax.broadcasted_iota(jnp.int32, (HEAD, LANES), 1) & (FIELD - 1)
    sub = lax.broadcasted_iota(jnp.int32, (HEAD, LANES), 0)
    tail_mask = lane == HEAD + (sub & (TAIL - 1))
    for b in range(n):
        at = (b // half) * half * CAP
        k = b % half
        head = jnp.where(lane == sub, table[at + k * HEAD:at + (k + 1) * HEAD], 0.0)
        first = at + half * HEAD + k * TAIL
        tile, place = first // HEAD * HEAD, first % HEAD
        inside = tail_mask & (sub >= place) & (sub < place + TAIL)
        line = head + jnp.where(inside, table[tile:tile + HEAD], 0.0)
        out_ref[pl.ds(me ^ owners[b], 1), :] = jnp.sum(line, axis=0, keepdims=True)


def row_stats(owners, near, far, weight):
    n = len(owners)
    width, vocab_dev = weight.shape
    return pl.pallas_call(
        functools.partial(stats_kernel, owners, 256),
        out_shape=pltpu.VMEM((n, LANES), jnp.float32),
        in_specs=[VMEM] * 3,
        out_specs=VMEM,
        scratch_shapes=[pltpu.VMEM((n * CAP, vocab_dev), jnp.float32)],
        compiler_params=pltpu.CompilerParams(vmem_limit_bytes=16 * MIB),
        name="row_stats",
    )(near, far, weight)


def finish_kernel(lines_ref, scored_ref, logprob_ref, entropy_ref):
    slots = logprob_ref.shape[0]
    lines = lines_ref[...]
    peak = jnp.max(lines, axis=0, keepdims=True)
    factor = jnp.exp(lines - peak)

    def field(k):
        return pltpu.roll(lines, LANES - FIELD * k, 1)

    total = jnp.sum(field(1) * factor, axis=0, keepdims=True)
    moment = jnp.sum(field(2) * factor, axis=0, keepdims=True)
    chosen = jnp.sum(field(3), axis=0, keepdims=True)
    log_total = jnp.log(total)
    scored = scored_ref[0:1] > 0.0
    logprob = jnp.where(scored, chosen - peak - log_total, 0.0)
    entropy = jnp.where(scored, peak + log_total - moment / total, 0.0)
    logprob_ref[...] = logprob[0, :slots]
    entropy_ref[...] = entropy[0, :slots]


def finish(lines, scored, slots):
    return pl.pallas_call(
        finish_kernel,
        out_shape=(jax.ShapeDtypeStruct((slots,), jnp.float32),) * 2,
        in_specs=[VMEM] * 2,
        out_specs=[VMEM] * 2,
        compiler_params=pltpu.CompilerParams(vmem_limit_bytes=4 * MIB),
        name="finish",
    )(lines, scored)


def on_device(n, hidden, norm_gain, head_weight, targets, counts):
    slots, width = hidden.shape
    block, scored = front(hidden, norm_gain, targets, counts)
    blocks, owners = [block], [0]
    *steps, last = gather_masks(n)
    for masks in steps:
        got = [swap(b, mask, n) for mask in masks for b in blocks]
        owners = owners + [o ^ mask for mask in masks for o in owners]
        blocks = blocks + got
    weight = fetch(blocks[len(blocks) // 2 - 1], head_weight)
    weight, *blocks = lax.optimization_barrier((weight, *blocks))
    near = unpack(blocks, width)
    far = swap(near, last[0], n)
    owners = owners + [o ^ last[0] for o in owners]
    lines = row_stats(tuple(owners), near, far, weight)
    lines = lax.all_to_all(lines, "vocab", 0, 0, tiled=True)
    return finish(lines, scored, slots)


def solution(mesh):
    n = mesh.shape["vocab"]
    in_specs = (
        P(("req", "vocab"), None),
        P(),
        P(None, "vocab"),
        P(("req", "vocab")),
        P(("req", "vocab")),
    )
    out_specs = (P(("req", "vocab")), P(("req", "vocab")))

    def step(*args):
        return on_device(n, *args)

    return jax.shard_map(step, mesh=mesh, in_specs=in_specs, out_specs=out_specs, check_vma=False)
```

time: 36.6 us -> 31.9 us (0.87)
  blocking collectives: 0 us -> 11.2 us
  waiting for transfers between devices: 12.9 us -> 5.04 us
  starting transfers between devices: 14.3 us -> 8.75 us
  local copies, waits for them, and re-layouts: 3.24 us -> 0 us
  Pallas kernels: 3.51 us -> 5.38 us
  other arithmetic: 1.02 us -> 0 us
    all_to_all x0 -> x1, blocking collectives: none -> 11.2 us  [on_device(): lines = lax.all_to_all(lines, 'vocab', 0, 0, tiled=True)]
    all_to_all x1 -> x0, waiting for transfers between devices: 7.29 us -> none  [on_device(): back = lax.all_to_all(stats, 'vocab', 0, 0, tiled=True)]
    all_to_all x1 -> x0, starting transfers between devices: 5.03 us -> none  [on_device(): back = lax.all_to_all(stats, 'vocab', 0, 0, tiled=True)]
    unnamed x9 -> x0, local copies, waits for them, and re-layouts: 3.23 us -> none
    pallas_call x2 -> x5, Pallas kernels: 3.51 us -> 5.38 us  [the longest x1 2.38 us: fetch(): pl.pallas_call(fetch_kernel, out_shape=pltpu.VMEM(weight.shape, weight.dt...]
    ppermute x8, starting transfers between devices: 9.31 us -> 8.75 us  [swap(): return lax.ppermute(block, 'vocab', [(i, i ^ mask) for i in range(n)])]
    ppermute x8, waiting for transfers between devices: 5.59 us -> 5.04 us  [swap(): return lax.ppermute(block, 'vocab', [(i, i ^ mask) for i in range(n)])]
    select_n x1 -> x0, other arithmetic: 0.53 us -> none  [on_device(): jnp.where(scored, peak + log_total - moment / total, jnp.float32(0.0))]
  transfers between devices with their start and end apart: 9 -> 8, of which waited for: 6 -> 3; matrix products, arithmetic and copies ran while one was open for 2% -> 0% of each run, Pallas kernels for 0% -> 7%
where the time goes in v3:
time: 31.9 us; the launch traced here: 31.7 us
  blocking collectives  11.2 us (35%)
  starting transfers between devices  8.75 us (27%)
  Pallas kernels  5.38 us (17%)
  waiting for transfers between devices  5.04 us (16%)
  between operations  1.34 us (4%)
    all_to_all x1, blocking collectives, on_device(): lines = lax.all_to_all(lines, 'vocab', 0, 0, tiled=True)  11.2 us
    ppermute x8, starting transfers between devices, swap(): return lax.ppermute(block, 'vocab', [(i, i ^ mask) for i in range(n)])  8.75 us
    ppermute x8, waiting for transfers between devices, swap(): return lax.ppermute(block, 'vocab', [(i, i ^ mask) for i in range(n)])  5.04 us
    pallas_call x1, Pallas kernels, fetch(): pl.pallas_call(fetch_kernel, out_shape=pltpu.VMEM(weight.shape, weight.dt...  2.38 us
    pallas_call x1, Pallas kernels, row_stats(): pl.pallas_call(functools.partial(stats_kernel, owners, 256), out_shape=pl...  1.28 us
    pallas_call x1, Pallas kernels, front(): pl.pallas_call(front_kernel, out_shape=(pltpu.VMEM((HEAD, tiles * LANES),...  1.03 us
  transfers between devices with their start and end apart: 8, of which 3 were waited for; matrix products, arithmetic and copies ran while one was open for 0% of the time, Pallas kernels for 7%

profile of v3, /device:TPU:0, one launch (start us, length us, event | category | flops | bytes accessed | tf_op | source)
XLA Modules:
  0.0 31.7 jit_solution(8793662162128326691)
XLA Ops:
  1.3 1.0 %norm_and_pack.1 = (bf16[8,3072]{1,0:T(8,128)(2,1)S(1)}, f32[8,128]{1,0:T(8,128)S(1)}) custom-call(bf16[16,2304]{1,0:T(8,128)(2,1)} %hidden_hbm.1, f32[2304]{0:T(1024)} %gain_hbm.1, s32[16]{0:T(128)} %targets_hbm.1, s32[1]{0:T(128)S(6)} %copy.8.counts_ref), custom_call_target="tpu_custom_call" | custom-call | tf_op jit(solution)/shard_map/norm_and_pack/pallas_call | solution.py:84
  2.3 2.5 %collective-permute-start.2 = (bf16[8,3072]{1,0:T(8,128)(2,1)S(1)}, bf16[8,3072]{1,0:T(8,128)(2,1)S(1)}, u32[]{:S(2)}, u32[]{:S(2)}) collective-permute-start(bf16[8,3072]{1,0:T(8,128)(2,1)S(1)} %get-tuple-element.14.refs_0_), channel_id=1, source_target_pairs={{0,5},{1,4},{2,7},{3,6},{4,1},{5,0},{6,3},{7,2},{8,13},{9,12},{10,... | collective-permute-start | bytes 147464 | tf_op jit(solution)/shard_map/ppermute | solution.py:33
  4.8 2.6 %collective-permute-start.1 = (bf16[8,3072]{1,0:T(8,128)(2,1)S(1)}, bf16[8,3072]{1,0:T(8,128)(2,1)S(1)}, u32[]{:S(2)}, u32[]{:S(2)}) collective-permute-start(bf16[8,3072]{1,0:T(8,128)(2,1)S(1)} %get-tuple-element.14.refs_0_), channel_id=1, source_target_pairs={{0,8},{1,9},{2,10},{3,11},{4,12},{5,13},{6,14},{7,15},{8,0},{9,1},... | collective-permute-start | bytes 147464 | tf_op jit(solution)/shard_map/ppermute | solution.py:33
  7.4 0.2 collective-permute-start
  7.6 1.5 %collective-permute-start.3 = (bf16[8,3072]{1,0:T(8,128)(2,1)S(1)}, bf16[8,3072]{1,0:T(8,128)(2,1)S(1)}, u32[]{:S(2)}, u32[]{:S(2)}) collective-permute-start(bf16[8,3072]{1,0:T(8,128)(2,1)S(1)} %get-tuple-element.14.refs_0_), channel_id=1, source_target_pairs={{0,3},{1,2},{2,1},{3,0},{4,7},{5,6},{6,5},{7,4},{8,11},{9,10},{10,... | collective-permute-start | bytes 147464 | tf_op jit(solution)/shard_map/ppermute | solution.py:33
  9.1 0.0 collective-permute-done.2.refs_2_
  9.1 0.3 collective-permute-start.5
  9.4 1.8 %collective-permute-done.1.refs_1_ = bf16[8,3072]{1,0:T(8,128)(2,1)S(1)} collective-permute-done((bf16[8,3072]{1,0:T(8,128)(2,1)S(1)}, bf16[8,3072]{1,0:T(8,128)(2,1)S(1)}, u32[]{:S(2)}, u32[]{:S(2)}) %collective-permute-start.1) | collective-permute-done | bytes 49184 | tf_op jit(solution)/shard_map/ppermute | solution.py:33
  11.2 0.0 collective-permute-start.4
  11.2 1.6 %collective-permute-done.after_ref.refs_3_ = bf16[8,3072]{1,0:T(8,128)(2,1)S(1)} collective-permute-done((bf16[8,3072]{1,0:T(8,128)(2,1)S(1)}, bf16[8,3072]{1,0:T(8,128)(2,1)S(1)}, u32[]{:S(2)}, u32[]{:S(2)}) %collective-permute-start) | collective-permute-done | bytes 49184 | tf_op jit(solution)/shard_map/ppermute | solution.py:33
  12.8 1.6 %collective-permute-start.6 = (bf16[8,3072]{1,0:T(8,128)(2,1)S(1)}, bf16[8,3072]{1,0:T(8,128)(2,1)S(1)}, u32[]{:S(2)}, u32[]{:S(2)}) collective-permute-start(bf16[8,3072]{1,0:T(8,128)(2,1)S(1)} %collective-permute-done.after_ref.refs_3_), channel_id=1, source_target_pairs={{0,3},{1,2},{2,1},{3,0},{4,7},{5,6},{6,5},{7,4},{8,11},{9,10},{10,... | collective-permute-start | bytes 147464 | tf_op jit(solution)/shard_map/ppermute | solution.py:33
  14.3 2.4 %fetch_weights.1.weight_ref = bf16[2304,1024]{1,0:T(8,128)(2,1)S(1)} custom-call(bf16[8,3072]{1,0:T(8,128)(2,1)S(1)} %collective-permute-done.after_ref.refs_3_, bf16[2304,1024]{1,0:T(8,128)(2,1)} %weight_ref.1), custom_call_target="tpu_custom_call" | custom-call | bytes 4718592 | tf_op jit(solution)/shard_map/fetch_weights/pallas_call | solution.py:115
  16.7 0.0 collective-permute-done.3.refs_4_
  16.7 0.0 collective-permute-done.5.refs_6_
  16.7 0.0 collective-permute-done.4.refs_5_
  16.7 0.0 collective-permute-done.6.refs_7_
  16.7 0.1 unpack.1.near_ref
  16.8 0.1 collective-permute-start.7
  17.0 1.6 %collective-permute-done.7.far_ref = bf16[80,2432]{1,0:T(8,128)(2,1)S(1)} collective-permute-done((bf16[80,2432]{1,0:T(8,128)(2,1)S(1)}, bf16[80,2432]{1,0:T(8,128)(2,1)S(1)}, u32[]{:S(2)}, u32[]{:S(2)}) %collective-permute-start.7) | collective-permute-done | bytes 389152 | tf_op jit(solution)/shard_map/ppermute | solution.py:33
  18.6 1.3 %row_stats.1 = f32[16,128]{1,0:T(8,128)S(1)} custom-call(bf16[80,2432]{1,0:T(8,128)(2,1)S(1)} %unpack.1.near_ref, bf16[80,2432]{1,0:T(8,128)(2,1)S(1)} %collective-permute-done.7.far_ref, bf16[2304,1024]{1,0:T(8,128)(2,1)S(1)} %fetch_weights.1.weight_ref), custom_call_target="tpu_custom_call" | custom-call | tf_op jit(solution)/shard_map/row_stats/pallas_call | solution.py:198
  19.9 11.2 %all_to_all.11 = f32[16,1,128]{2,1,0:T(1,128)S(1)} all-to-all(f32[16,1,128]{2,1,0:T(1,128)S(1)} %bitcast.4), channel_id=1, replica_groups=mesh['req'=2,'vocab'=16] {'vocab'}, dimensions={0} | all-to-all | bytes 16384 | tf_op jit(solution)/shard_map/all_to_all | solution.py:255
  31.1 0.6 %finish.1 = (f32[16]{0:T(128)}, f32[16]{0:T(128)}) custom-call(f32[16,128]{1,0:T(8,128)S(1)} %bitcast.5, f32[8,128]{1,0:T(8,128)S(1)} %get-tuple-element.23.scored_ref), custom_call_target="tpu_custom_call" | custom-call | tf_op jit(solution)/shard_map/finish/pallas_call | solution.py:230
Async XLA Ops:
  2.3 6.8 %collective-permute-start.2 = (bf16[8,3072]{1,0:T(8,128)(2,1)S(1)}, bf16[8,3072]{1,0:T(8,128)(2,1)S(1)}, u32[]{:S(2)}, u32[]{:S(2)}) collective-permute-start(bf16[8,3072]{1,0:T(8,128)(2,1)S(1)} %get-tuple-element.14.refs_0_), channel_id=1, source_target_pairs={{0,5},{1,4},{2,7},{3,6},{4,1},{5,0},{6,3},{7,2},{8,13},{9,12},{10,... | collective-permute-start | bytes 147464 | tf_op jit(solution)/shard_map/ppermute | solution.py:33
  4.8 6.3 %collective-permute-start.1 = (bf16[8,3072]{1,0:T(8,128)(2,1)S(1)}, bf16[8,3072]{1,0:T(8,128)(2,1)S(1)}, u32[]{:S(2)}, u32[]{:S(2)}) collective-permute-start(bf16[8,3072]{1,0:T(8,128)(2,1)S(1)} %get-tuple-element.14.refs_0_), channel_id=1, source_target_pairs={{0,8},{1,9},{2,10},{3,11},{4,12},{5,13},{6,14},{7,15},{8,0},{9,1},... | collective-permute-start | bytes 147464 | tf_op jit(solution)/shard_map/ppermute | solution.py:33
  7.4 5.3 %collective-permute-start = (bf16[8,3072]{1,0:T(8,128)(2,1)S(1)}, bf16[8,3072]{1,0:T(8,128)(2,1)S(1)}, u32[]{:S(2)}, u32[]{:S(2)}) collective-permute-start(bf16[8,3072]{1,0:T(8,128)(2,1)S(1)} %get-tuple-element.14.refs_0_), channel_id=1, source_target_pairs={{0,13},{1,12},{2,15},{3,14},{4,9},{5,8},{6,11},{7,10},{8,5},{9,4},... | collective-permute-start | bytes 147464 | tf_op jit(solution)/shard_map/ppermute | solution.py:33
  7.6 9.1 %collective-permute-start.3 = (bf16[8,3072]{1,0:T(8,128)(2,1)S(1)}, bf16[8,3072]{1,0:T(8,128)(2,1)S(1)}, u32[]{:S(2)}, u32[]{:S(2)}) collective-permute-start(bf16[8,3072]{1,0:T(8,128)(2,1)S(1)} %get-tuple-element.14.refs_0_), channel_id=1, source_target_pairs={{0,3},{1,2},{2,1},{3,0},{4,7},{5,6},{6,5},{7,4},{8,11},{9,10},{10,... | collective-permute-start | bytes 147464 | tf_op jit(solution)/shard_map/ppermute | solution.py:33
  9.1 7.6 %collective-permute-start.5 = (bf16[8,3072]{1,0:T(8,128)(2,1)S(1)}, bf16[8,3072]{1,0:T(8,128)(2,1)S(1)}, u32[]{:S(2)}, u32[]{:S(2)}) collective-permute-start(bf16[8,3072]{1,0:T(8,128)(2,1)S(1)} %collective-permute-done.2.refs_2_), channel_id=1, source_target_pairs={{0,3},{1,2},{2,1},{3,0},{4,7},{5,6},{6,5},{7,4},{8,11},{9,10},{10,... | collective-permute-start | bytes 147464 | tf_op jit(solution)/shard_map/ppermute | solution.py:33
  11.2 5.6 %collective-permute-start.4 = (bf16[8,3072]{1,0:T(8,128)(2,1)S(1)}, bf16[8,3072]{1,0:T(8,128)(2,1)S(1)}, u32[]{:S(2)}, u32[]{:S(2)}) collective-permute-start(bf16[8,3072]{1,0:T(8,128)(2,1)S(1)} %collective-permute-done.1.refs_1_), channel_id=1, source_target_pairs={{0,3},{1,2},{2,1},{3,0},{4,7},{5,6},{6,5},{7,4},{8,11},{9,10},{10,... | collective-permute-start | bytes 147464 | tf_op jit(solution)/shard_map/ppermute | solution.py:33
  12.8 4.0 %collective-permute-start.6 = (bf16[8,3072]{1,0:T(8,128)(2,1)S(1)}, bf16[8,3072]{1,0:T(8,128)(2,1)S(1)}, u32[]{:S(2)}, u32[]{:S(2)}) collective-permute-start(bf16[8,3072]{1,0:T(8,128)(2,1)S(1)} %collective-permute-done.after_ref.refs_3_), channel_id=1, source_target_pairs={{0,3},{1,2},{2,1},{3,0},{4,7},{5,6},{6,5},{7,4},{8,11},{9,10},{10,... | collective-permute-start | bytes 147464 | tf_op jit(solution)/shard_map/ppermute | solution.py:33
  16.8 1.8 %collective-permute-start.7 = (bf16[80,2432]{1,0:T(8,128)(2,1)S(1)}, bf16[80,2432]{1,0:T(8,128)(2,1)S(1)}, u32[]{:S(2)}, u32[]{:S(2)}) collective-permute-start(bf16[80,2432]{1,0:T(8,128)(2,1)S(1)} %unpack.1.near_ref), channel_id=1, source_target_pairs={{0,1},{1,0},{2,3},{3,2},{4,5},{5,4},{6,7},{7,6},{8,9},{9,8},{10,11... | collective-permute-start | bytes 1167368 | tf_op jit(solution)/shard_map/ppermute | solution.py:33
